TPU v7x, 256 devices: a whole 4x4x8 slice. The times are simulated.
256 devices in a mesh: ctx: 64 (over x, z, core), head: 4 (over y).
Axes of the slice: x: 4, y: 4, z: 8, core: 2. Of those that a mesh axis runs over, the one named last changes fastest.
Arguments:
- queries: bfloat16 [16384, 2560], P('ctx', 'head'), may hold values from -8 to 8
- key_tokens: bfloat16 [16384, 2560], P('ctx', 'head'), may hold values from -8 to 8
- value_tokens: bfloat16 [16384, 2560], P('ctx', 'head'), may hold values from -8 to 8
- pair_keys: int32 [512, 4], P('ctx'), may hold values from 0 to 511, as said below
- pair_count: int32 [512], P('ctx'), may hold values from 1 to 4, as said below
Outputs:
- attended: bfloat16 [16384, 2560], P('ctx', 'head')
Inputs may be any that keep to these rules, and one draw needn't show every extreme that they name: `pair_keys`: the 4 entries of a row are distinct, padded slots too. Key block c lies on index c // 8 of ctx. Among all 4 slots (padded ones included) of the 8 rows of one index of ctx, at most 2 name key blocks of any one index, its own included, and on every index some one index is named exactly 2 times. `pair_count`: every index of ctx has a query block whose count is 4.
All inputs are finite; a program needn't handle non-finite values.
Results may differ from a plain program's by a relative error of at most 0.0059.
Values may be sent and summed in bfloat16 or wider, within the bound.
No kernel may reach another device: no remote copies, remote signals or barrier semaphores. Data moves between devices by JAX's collectives and lax.ppermute only.
A program may use at most 128 MiB of HBM per device.

v0:
```python
import math

import jax
import jax.numpy as jnp
from jax import lax
from jax.sharding import PartitionSpec as P

HD = 128
BLOCK = 32


NEGATIVE = -1e30


def absorb(running, logits, kept_mask, weighted):
    row_max, denominator, numerator = running
    logits = jnp.where(kept_mask, logits, NEGATIVE)
    fresh_max = jnp.maximum(row_max, jnp.max(logits, axis=-1))
    weights = jnp.where(kept_mask, jnp.exp(logits - fresh_max[..., None]), 0.0)
    denominator = jnp.sum(weights, axis=-1)
    numerator = weighted(weights.astype(jnp.bfloat16))
    return (fresh_max, denominator, numerator)


def body(queries, key_tokens, value_tokens, pair_keys, pair_count):
    tok_rows, columns = queries.shape
    head_count = columns // HD
    block_count = tok_rows // BLOCK
    pair_slots = pair_keys.shape[1]
    device_count = lax.axis_size("ctx")
    inv_root = 1.0 / math.sqrt(HD)
    query_four = queries.reshape(block_count, BLOCK, head_count, HD)
    key_blocks = key_tokens.reshape(block_count, BLOCK, columns)
    value_blocks = value_tokens.reshape(block_count, BLOCK, columns)
    key_means = jnp.mean(key_blocks.astype(jnp.float32), axis=1).astype(jnp.bfloat16)
    value_means = jnp.mean(value_blocks.astype(jnp.float32), axis=1).astype(jnp.bfloat16)
    usable = jnp.arange(pair_slots, dtype=jnp.int32)[None, :] < pair_count[:, None]
    initial = (
        jnp.full((head_count, block_count, BLOCK), NEGATIVE, jnp.float32),
        jnp.zeros((head_count, block_count, BLOCK), jnp.float32),
        jnp.zeros((block_count, BLOCK, head_count, HD), jnp.float32),
    )
    running = initial
    mean_keys = lax.all_gather(key_means, "ctx", axis=0, tiled=True)
    mean_values = lax.all_gather(value_means, "ctx", axis=0, tiled=True)
    row_total = mean_keys.shape[0]
    last_row = min(row_total, 512)
    part_keys = mean_keys.reshape(last_row, head_count, HD)
    part_values = mean_values.reshape(last_row, head_count, HD)
    logits = jnp.einsum(
        "bthd,chd->hbtc", query_four, part_keys, preferred_element_type=jnp.float32
    ) * inv_root + math.log(BLOCK)
    block_ids = jnp.arange(last_row, dtype=jnp.int32)
    refined_mask = jnp.any(
        (pair_keys[:, :, None] == block_ids[None, None, :]) & usable[:, :, None], axis=1
    )
    kept_mask = jnp.logical_not(refined_mask)[None, :, None, :]

    def weighted(weights, part_values=part_values):
        return jnp.einsum(
            "hbtc,chd->bthd", weights, part_values, preferred_element_type=jnp.float32
        )

    running = absorb(running, logits, kept_mask, weighted)
    owners = (pair_keys // block_count).reshape(-1)
    within = (pair_keys % block_count).reshape(-1)
    capacity = max(2, (5 * block_count * pair_slots + 4 * device_count - 1) // (4 * device_count))
    owner_hits = (owners[:, None] == jnp.arange(device_count, dtype=jnp.int32)[None, :]).astype(
        jnp.int32
    )
    position = jnp.sum(jnp.cumsum(owner_hits, axis=0) * owner_hits, axis=1) - 1
    requests = jnp.zeros((device_count, capacity), jnp.int32).at[owners, position].set(within)
    key_value = jnp.stack((key_blocks, value_blocks), axis=1)
    slot_index = (
        jnp.zeros((device_count, capacity), jnp.int32)
        .at[owners, position]
        .set(jnp.arange(block_count * pair_slots, dtype=jnp.int32))
    )
    query_slots = queries.reshape(block_count, BLOCK, columns)[slot_index // pair_slots]
    asked_queries = lax.all_to_all(query_slots, "ctx", split_axis=0, concat_axis=0, tiled=True)
    requested = lax.all_to_all(requests, "ctx", split_axis=0, concat_axis=0, tiled=True)
    item_count = requested.shape[1]
    local_blocks = key_value[requested]
    local_queries = asked_queries.reshape(device_count, item_count, BLOCK, head_count, HD)
    local_keys = local_blocks[:, :, 0].reshape(device_count, item_count, BLOCK, head_count, HD)
    local_values = local_blocks[:, :, 1].reshape(device_count, item_count, BLOCK, head_count, HD)
    logits = (
        jnp.einsum(
            "nithd,niuhd->nihtu", local_queries, local_keys, preferred_element_type=jnp.float32
        )
        * inv_root
    )
    part_max = jnp.max(logits, axis=-1)
    weights = jnp.exp(logits - part_max[..., None])
    part_sum = jnp.sum(weights, axis=-1)
    part_values = jnp.einsum(
        "nihtu,niuhd->nithd",
        weights.astype(jnp.bfloat16),
        local_values,
        preferred_element_type=jnp.float32,
    )
    part_values = part_values.reshape(device_count, item_count, BLOCK, columns)
    part_values, part_max, part_sum = (
        lax.all_to_all(part_values, "ctx", split_axis=0, concat_axis=0, tiled=True),
        lax.all_to_all(part_max, "ctx", split_axis=0, concat_axis=0, tiled=True),
        lax.all_to_all(part_sum, "ctx", split_axis=0, concat_axis=0, tiled=True),
    )
    slot_values = part_values[owners, position].reshape(
        block_count, pair_slots, BLOCK, head_count, HD
    )
    slot_max = jnp.transpose(
        part_max[owners, position].reshape(block_count, pair_slots, head_count, BLOCK), (2, 0, 3, 1)
    )
    slot_sum = jnp.transpose(
        part_sum[owners, position].reshape(block_count, pair_slots, head_count, BLOCK), (2, 0, 3, 1)
    )
    kept_slot = usable[None, :, None, :]
    row_max, denominator, numerator = running
    slot_max = jnp.where(kept_slot, slot_max, NEGATIVE)
    fresh_max = jnp.maximum(row_max, jnp.max(slot_max, axis=-1))
    rescale = jnp.exp(row_max - fresh_max)
    slot_ratio = jnp.where(kept_slot, jnp.exp(slot_max - fresh_max[..., None]), 0.0)
    denominator = denominator * rescale + jnp.sum(slot_ratio * slot_sum, axis=-1)
    scaled = jnp.transpose(slot_ratio, (1, 3, 2, 0))[..., None] * slot_values
    numerator = numerator * jnp.transpose(rescale, (1, 2, 0))[..., None] + jnp.sum(scaled, axis=1)
    attended = numerator / jnp.transpose(denominator, (1, 2, 0))[..., None]
    return attended.reshape(tok_rows, columns).astype(jnp.bfloat16)


def solution(mesh):
    placed = (P("ctx", "head"), P("ctx", "head"), P("ctx", "head"), P("ctx", None), P("ctx"))
    return jax.shard_map(
        body, mesh=mesh, in_specs=placed, out_specs=P("ctx", "head"), check_vma=False
    )
```

profile of v0, /device:TPU:8, one launch (start us, length us, event | category | flops | bytes accessed | tf_op | source)
XLA Modules:
  0.0 585.3 jit_solution(13188625025002449695)
XLA Ops:
  0.0 0.7 add_select_fusion
  0.7 0.1 copy.148
  0.8 0.1 eq.33
  1.1 0.2 select_reduce_fusion
  1.3 0.1 copy.151
  1.4 0.1 reshape.228
  1.5 2.0 scatter_fusion.1
  3.5 0.7 copy.152
  4.2 11.9 %all-to-all-start.1 = ((s32[64,1,2]{2,1,0:T(1,128)}), s32[64,1,2]{2,1,0:T(1,128)S(1)}, u32[]{:S(2)}, u32[]{:S(2)}) async-start(s32[64,1,2]{2,1,0:T(1,128)} %copy.152), calls=%async_computation.1 | async-start | bytes 65536 | tf_op jit(solution)/shard_map/all_to_all | solution.py:81
  16.2 2.0 scatter_fusion
  18.2 0.1 copy.150
  18.3 0.1 reshape.188
  18.5 3.5 gather_fusion
  22.0 3.6 all-to-all-done.1
  25.6 7.1 %all-to-all-start = ((bf16[64,2,32,640]{3,2,1,0:T(8,128)(2,1)}), bf16[64,2,32,640]{3,2,1,0:T(8,128)(2,1)}, u32[]{:S(2)}, u32[]{:S(2)}) async-start(bf16[64,2,32,640]{3,2,1,0:T(8,128)(2,1)} %bitcast.157), calls=%async_computation | async-start | bytes 10485760 | tf_op jit(solution)/shard_map/all_to_all | solution.py:80
  32.9 0.1 copy.154
  33.0 0.1 reshape.196
  33.2 7.4 %gather_fusion.1 = bf16[128,2,32,640]{3,2,1,0:T(8,128)(2,1)} fusion(bf16[8,2,32,640]{3,2,0,1:T(8,128)(2,1)S(1)} %pad_maximum_fusion, s32[1024]{0:T(1024)S(1)} %pad_clamp_fusion), kind=kCustom, calls=%fused_computation.1 | custom fusion | bytes 20972032 | tf_op jit(solution)/shard_map/gather | solution.py:83
  40.6 9.0 %copy.155 = bf16[128,2,32,640]{3,2,0,1:T(8,128)(2,1)} copy(bf16[128,2,32,640]{3,2,1,0:T(8,128)(2,1)} %gather_fusion.1) | data formatting | bytes 20971520 | tf_op jit(solution)/shard_map/gather | solution.py:83
  49.6 9.1 %fusion.57 = (bf16[64,2,1,32,640]{4,3,1,0,2:T(8,128)(2,1)}, bf16[64,2,1,32,640]{4,3,1,0,2:T(8,128)(2,1)}) fusion(bf16[64,2,2,32,640]{4,3,1,0,2:T(8,128)(2,1)} %bitcast.153), kind=kLoop, calls=%fused_computation.91 | loop fusion | bytes 20971520 | tf_op jit(solution)/shard_map/slice | solution.py:86
  58.7 13.1 %reshape_squeeze.6 = bf16[64,2,32,5,128]{4,3,2,1,0:T(8,128)(2,1)} reshape(bf16[64,2,1,32,640]{4,3,1,0,2:T(8,128)(2,1)} %get-tuple-element.11) | data formatting | bytes 10485760 | tf_op jit(solution)/shard_map/reshape;squeeze | solution.py:85
  71.8 79.1 %all-to-all-done = bf16[64,2,32,640]{3,2,1,0:T(8,128)(2,1)} async-done(((bf16[64,2,32,640]{3,2,1,0:T(8,128)(2,1)}), bf16[64,2,32,640]{3,2,1,0:T(8,128)(2,1)}, u32[]{:S(2)}, u32[]{:S(2)}) %all-to-all-start) | async-done | bytes 5242912 | tf_op jit(solution)/shard_map/all_to_all | solution.py:80
  150.8 11.7 %multiply_reduce_fusion = (f32[64,2,5,32]{3,2,1,0:T(8,128)S(1)}, f32[64,2,5,32,32]{3,4,2,1,0:T(8,128)}) fusion(bf16[64,2,32,5,128]{4,3,2,1,0:T(8,128)(2,1)} %reshape_squeeze.6, bf16[64,2,32,640]{3,2,1,0:T(8,128)(2,1)} %all-to-all-done), kind=kOutput, calls=%fused_computation.9 | convolution fusion | flops 169062400 | bytes 13189120 | tf_op jit(solution)/shard_map/nithd,niuhd->nihtu/dot_general | solution.py:88
  162.5 7.1 %fusion = f32[64,2,5,32]{3,2,1,0:T(8,128)S(1)} fusion(f32[64,2,5,32,32]{3,4,2,1,0:T(8,128)} %get-tuple-element.17, f32[64,2,5,32]{3,2,1,0:T(8,128)S(1)} %get-tuple-element.16), kind=kLoop, calls=%fused_computation.10 | loop fusion | flops 1945600 | bytes 2785280 | tf_op jit(solution)/shard_map/reduce_sum | solution.py:95
  169.6 0.2 copy.206
  169.8 1.0 reshape.240
  170.7 6.0 %all-to-all-start.4 = ((f32[64,1,320]{2,1,0:T(1,128)}), f32[64,1,320]{2,1,0:T(1,128)S(1)}, u32[]{:S(2)}, u32[]{:S(2)}) async-start(f32[64,1,320]{2,1,0:T(1,128)} %reshape.240), calls=%async_computation.4 | async-start | bytes 196608 | tf_op jit(solution)/shard_map/all_to_all | solution.py:106
  176.7 12.6 %reshape_squeeze.7 = bf16[64,2,32,5,128]{4,3,2,1,0:T(8,128)(2,1)} reshape(bf16[64,2,1,32,640]{4,3,1,0,2:T(8,128)(2,1)} %get-tuple-element.10) | data formatting | bytes 10485760 | tf_op jit(solution)/shard_map/reshape;squeeze | solution.py:86
  189.4 0.2 copy.207
  189.5 1.0 reshape.238
  190.5 10.5 %all-to-all-start.2 = ((f32[64,1,320]{2,1,0:T(1,128)}), f32[64,1,320]{2,1,0:T(1,128)S(1)}, u32[]{:S(2)}, u32[]{:S(2)}) async-start(f32[64,1,320]{2,1,0:T(1,128)} %reshape.238), calls=%async_computation.2 | async-start | bytes 196608 | tf_op jit(solution)/shard_map/all_to_all | solution.py:105
  201.0 12.8 %fusion.11 = f32[64,2,5,4,8,128]{5,4,3,2,1,0:T(8,128)} fusion(f32[64,2,5,32,32]{3,4,2,1,0:T(8,128)} %get-tuple-element.17, f32[64,2,5,32]{3,2,1,0:T(8,128)S(1)} %get-tuple-element.16, bf16[64,2,32,5,128]{4,3,2,1,0:T(8,128)(2,1)} %reshape_squeeze.7), kind=kOutput, calls=%fused_computation.21 | convolution fusion | flops 169738240 | bytes 18432000 | tf_op jit(solution)/shard_map/nihtu,niuhd->nithd/dot_general | solution.py:96
  213.8 9.1 %copy.204 = f32[64,2,5,4,8,128]{5,4,2,3,1,0:T(8,128)} copy(f32[64,2,5,4,8,128]{5,4,3,2,1,0:T(8,128)} %fusion.11) | data formatting | bytes 20971520 | tf_op jit(solution)/shard_map/reshape | solution.py:102
  222.9 0.6 copy-done.4
  223.5 10.7 %all-to-all-start.3 = ((f32[64,2,32,640]{3,2,1,0:T(8,128)}), f32[64,2,32,640]{3,2,1,0:T(8,128)}, u32[]{:S(2)}, u32[]{:S(2)}) async-start(f32[64,2,32,640]{3,2,1,0:T(8,128)} %bitcast.152), calls=%async_computation.3 | async-start | bytes 20971520 | tf_op jit(solution)/shard_map/all_to_all | solution.py:104
  234.2 0.4 reshape.175
  234.7 0.1 copy.143
  234.8 0.1 fusion.44
  235.0 270.1 %all_gather.7 = bf16[512,640]{1,0:T(8,128)(2,1)S(1)} all-gather(bf16[8,640]{1,0:T(8,128)(2,1)S(1)} %multiply_convert_fusion), channel_id=1, replica_groups=mesh['ctx'=64,'head'=4] {'ctx'}, dimensions={0}, use_global_device_ids=true | all-gather | bytes 665600 | tf_op jit(solution)/shard_map/all_gather | solution.py:44
  505.0 0.2 copy.144
  505.3 0.8 copy.146
  506.2 49.7 %all_gather.6 = bf16[512,640]{1,0:T(8,128)(2,1)S(1)} all-gather(bf16[8,640]{1,0:T(8,128)(2,1)S(1)} %multiply_convert_fusion.1), channel_id=1, replica_groups=mesh['ctx'=64,'head'=4] {'ctx'}, dimensions={0}, use_global_device_ids=true | all-gather | bytes 665600 | tf_op jit(solution)/shard_map/all_gather | solution.py:45
  555.8 1.1 copy.142
  556.9 1.5 fusion.58
  558.4 0.5 fusion.18
  558.9 0.6 broadcast.303
  559.5 0.9 reduce.1
  560.4 0.2 reshape.241
  560.7 2.4 reduce
  563.1 1.1 reshape.239
  564.2 0.9 copy.159
  565.1 0.6 gather_fusion.4
  565.8 1.7 gather_fusion.2
  567.4 0.1 bitcast_reduce_fusion
  567.6 0.1 fusion.42
  567.7 1.0 fusion.16
  568.7 0.1 fusion.38
  568.9 0.3 copy.162
  569.2 6.2 %gather_fusion.3 = f32[32,32,640]{2,1,0:T(8,128)} fusion(f32[64,2,32,640]{3,2,1,0:T(8,128)} %all-to-all-done.3, s32[32]{0:T(128)S(1)} %bitcast.160), kind=kCustom, calls=%fused_computation.3 | custom fusion | bytes 5243136 | tf_op jit(solution)/shard_map/gather | solution.py:108
  575.3 4.4 reshape.182
  579.7 3.0 multiply_reduce_fusion.1
  582.7 1.3 fusion.34
  584.0 0.2 copy.172
  584.3 0.8 copy.205
  (40 shorter events, 0.8 us)
Async XLA Ops:
  0.0 18.5 %copy-start = (bf16[256,640]{1,0:T(8,128)(2,1)S(1)}, bf16[256,640]{1,0:T(8,128)(2,1)}, u32[]{:S(2)}) copy-start(bf16[256,640]{1,0:T(8,128)(2,1)} %param.5) | copy-start | bytes 983044
  4.2 21.4 %all-to-all-start.1 = ((s32[64,1,2]{2,1,0:T(1,128)}), s32[64,1,2]{2,1,0:T(1,128)S(1)}, u32[]{:S(2)}, u32[]{:S(2)}) async-start(s32[64,1,2]{2,1,0:T(1,128)} %copy.152), calls=%async_computation.1 | async-start | bytes 65536 | tf_op jit(solution)/shard_map/all_to_all | solution.py:81
  25.6 7.1 %copy-start.1 = (bf16[256,640]{1,0:T(8,128)(2,1)S(1)}, bf16[256,640]{1,0:T(8,128)(2,1)}, u32[]{:S(2)}) copy-start(bf16[256,640]{1,0:T(8,128)(2,1)} %param.6) | copy-start | bytes 983044
  25.6 7.1 %copy-start.2 = (bf16[256,640]{1,0:T(8,128)(2,1)S(1)}, bf16[256,640]{1,0:T(8,128)(2,1)}, u32[]{:S(2)}) copy-start(bf16[256,640]{1,0:T(8,128)(2,1)} %param.7) | copy-start | bytes 983044
  25.6 125.2 %all-to-all-start = ((bf16[64,2,32,640]{3,2,1,0:T(8,128)(2,1)}), bf16[64,2,32,640]{3,2,1,0:T(8,128)(2,1)}, u32[]{:S(2)}, u32[]{:S(2)}) async-start(bf16[64,2,32,640]{3,2,1,0:T(8,128)(2,1)} %bitcast.157), calls=%async_computation | async-start | bytes 10485760 | tf_op jit(solution)/shard_map/all_to_all | solution.py:80
  170.7 19.8 %all-to-all-start.4 = ((f32[64,1,320]{2,1,0:T(1,128)}), f32[64,1,320]{2,1,0:T(1,128)S(1)}, u32[]{:S(2)}, u32[]{:S(2)}) async-start(f32[64,1,320]{2,1,0:T(1,128)} %reshape.240), calls=%async_computation.4 | async-start | bytes 196608 | tf_op jit(solution)/shard_map/all_to_all | solution.py:106
  190.5 32.3 %all-to-all-start.2 = ((f32[64,1,320]{2,1,0:T(1,128)}), f32[64,1,320]{2,1,0:T(1,128)S(1)}, u32[]{:S(2)}, u32[]{:S(2)}) async-start(f32[64,1,320]{2,1,0:T(1,128)} %reshape.238), calls=%async_computation.2 | async-start | bytes 196608 | tf_op jit(solution)/shard_map/all_to_all | solution.py:105
  222.9 0.6 copy-start.4
  222.9 11.7 %copy-start.6 = (s32[8]{0:T(128)S(1)}, s32[8]{0:T(128)}, u32[]{:S(2)}) copy-start(s32[8]{0:T(128)} %param.9) | copy-start | bytes 100
  222.9 11.9 %copy-start.5 = (s32[8,4]{0,1:T(4,128)S(1)}, s32[8,4]{0,1:T(4,128)}, u32[]{:S(2)}) copy-start(s32[8,4]{0,1:T(4,128)} %param.8) | copy-start | bytes 388
  223.5 345.6 %all-to-all-start.3 = ((f32[64,2,32,640]{3,2,1,0:T(8,128)}), f32[64,2,32,640]{3,2,1,0:T(8,128)}, u32[]{:S(2)}, u32[]{:S(2)}) async-start(f32[64,2,32,640]{3,2,1,0:T(8,128)} %bitcast.152), calls=%async_computation.3 | async-start | bytes 20971520 | tf_op jit(solution)/shard_map/all_to_all | solution.py:104
  579.7 3.0 copy-start.3
where the time goes:
time: 595 us; the launch traced here: 585 us
  blocking collectives  320 us (54%)
  local copies, waits for them, and re-layouts  92.1 us (15%)
  waiting for transfers between devices  82.6 us (14%)
  starting transfers between devices  46.2 us (8%)
  matrix products  27.2 us (5%)
  other arithmetic  16.7 us (3%)
    all_gather x1, blocking collectives, body(): mean_keys = lax.all_gather(key_means, 'ctx', axis=0, tiled=True)  270 us
    all_to_all x1, waiting for transfers between devices, body(): lax.all_to_all(query_slots, 'ctx', split_axis=0, concat_axis=0, tiled=True)  79.1 us
    all_gather x1, blocking collectives, body(): mean_values = lax.all_gather(value_means, 'ctx', axis=0, tiled=True)  49.7 us
    gather x2, local copies, waits for them, and re-layouts, body(): local_blocks = key_value[requested]  16.4 us
    another operation x1, local copies, waits for them, and re-layouts, body(): local_blocks[:, :, 0]  13.1 us
    dot_general x1, matrix products, body(): jnp.einsum('nihtu,niuhd->nithd', weights.astype(jnp.bfloat16), local_valu...  12.8 us
    another operation x1, local copies, waits for them, and re-layouts, body(): local_blocks[:, :, 1]  12.6 us
    all_to_all x1, starting transfers between devices, body(): lax.all_to_all(requests, 'ctx', split_axis=0, concat_axis=0, tiled=True)  11.9 us
  transfers between devices with their start and end apart: 5, of which 2 were waited for; matrix products, arithmetic and copies ran while one was open for 16% of the time, Pallas kernels for 0%

commit v1 on v0

v1 whole, which is shorter than its diff:
```python
import math

import jax
import jax.numpy as jnp
from jax import lax
from jax.experimental import pallas as pl
from jax.experimental.pallas import tpu as pltpu
from jax.sharding import PartitionSpec as P

HD = 128
BLOCK = 32
NEGATIVE = -1e30


def attend_kernel(
    half_blocks,
    pair_slots,
    pk_ref,
    pc_ref,
    q_ref,
    got_ref,
    mk_ref,
    mv_ref,
    o_ref,
    bias_ref,
):
    half, head = pl.program_id(0), pl.program_id(1)
    coarse_keys = mk_ref.shape[0]
    rows = got_ref.shape[1]
    fine_keys = BLOCK * rows
    inv_root = 1.0 / math.sqrt(HD)

    @pl.when(head == 0)
    def _():
        block_ids = lax.broadcasted_iota(jnp.int32, (1, coarse_keys), 1)
        row_ids = lax.broadcasted_iota(jnp.int32, (1, fine_keys), 1) % rows
        for local in range(half_blocks):
            block = half * half_blocks + local
            count = pc_ref[block]
            coarse = jnp.full((1, coarse_keys), math.log(BLOCK), jnp.float32)
            for slot in range(pair_slots):
                hit = jnp.where(slot < count, pk_ref[block * pair_slots + slot], -1)
                coarse = jnp.where(block_ids == hit, NEGATIVE, coarse)
            kept = (row_ids >= local * pair_slots) & (row_ids < local * pair_slots + count)
            fine = jnp.where(kept, 0.0, NEGATIVE)
            where = pl.ds(local * BLOCK, BLOCK)
            bias_ref[where, :coarse_keys] = jnp.broadcast_to(coarse, (BLOCK, coarse_keys))
            bias_ref[where, coarse_keys:] = jnp.broadcast_to(fine, (BLOCK, fine_keys))

    queries = q_ref[...]
    fine_k = got_ref[:BLOCK].reshape(fine_keys, HD)
    fine_v = got_ref[BLOCK:].reshape(fine_keys, HD)
    contract = (((1,), (1,)), ((), ()))
    coarse = lax.dot_general(queries, mk_ref[...], contract, preferred_element_type=jnp.float32)
    fine = lax.dot_general(queries, fine_k, contract, preferred_element_type=jnp.float32)
    coarse = coarse * inv_root + bias_ref[:, :coarse_keys]
    fine = fine * inv_root + bias_ref[:, coarse_keys:]
    top = jnp.maximum(
        jnp.max(coarse, axis=1, keepdims=True), jnp.max(fine, axis=1, keepdims=True)
    )
    coarse = jnp.exp(coarse - top)
    fine = jnp.exp(fine - top)
    total = jnp.sum(coarse, axis=1, keepdims=True) + jnp.sum(fine, axis=1, keepdims=True)
    numerator = jnp.dot(
        coarse.astype(jnp.bfloat16), mv_ref[...], preferred_element_type=jnp.float32
    )
    numerator = numerator + jnp.dot(
        fine.astype(jnp.bfloat16), fine_v, preferred_element_type=jnp.float32
    )
    o_ref[...] = (numerator / total).astype(o_ref.dtype)


def attend(queries, got, means, pair_keys, pair_count):
    tok_rows, columns = queries.shape
    heads = columns // HD
    block_count, pair_slots = pair_keys.shape
    halves = 2
    half_rows = tok_rows // halves
    half_slots = got.shape[1] // halves
    coarse_keys = means.shape[0]
    keys = coarse_keys + BLOCK * half_slots
    grid_spec = pltpu.PrefetchScalarGridSpec(
        num_scalar_prefetch=2,
        grid=(halves, heads),
        in_specs=[
            pl.BlockSpec((half_rows, HD), lambda i, h, *_: (i, h)),
            pl.BlockSpec((2 * BLOCK, half_slots, HD), lambda i, h, *_: (0, i, h)),
            pl.BlockSpec((coarse_keys, HD), lambda i, h, *_: (0, h)),
            pl.BlockSpec((coarse_keys, HD), lambda i, h, *_: (0, heads + h)),
        ],
        out_specs=pl.BlockSpec((half_rows, HD), lambda i, h, *_: (i, h)),
        scratch_shapes=[pltpu.VMEM((half_rows, keys), jnp.float32)],
    )

    def kernel(*refs):
        attend_kernel(block_count // halves, pair_slots, *refs)

    return pl.pallas_call(
        kernel,
        grid_spec=grid_spec,
        out_shape=jax.ShapeDtypeStruct((tok_rows, columns), jnp.bfloat16),
        compiler_params=pltpu.CompilerParams(vmem_limit_bytes=32 * 1024 * 1024),
        cost_estimate=pl.CostEstimate(
            flops=4 * tok_rows * keys * columns,
            bytes_accessed=8 * 1024 * 1024,
            transcendentals=tok_rows * keys * heads,
        ),
    )(pair_keys.reshape(-1), pair_count, queries, got, means, means)


def body(queries, key_tokens, value_tokens, pair_keys, pair_count):
    tok_rows, columns = queries.shape
    block_count = tok_rows // BLOCK
    pair_slots = pair_keys.shape[1]
    devices = lax.axis_size("ctx")
    blocks = devices * block_count
    assert devices == 2 * BLOCK

    key_blocks = key_tokens.reshape(block_count, BLOCK, columns)
    value_blocks = value_tokens.reshape(block_count, BLOCK, columns)
    key_means = jnp.mean(key_blocks.astype(jnp.float32), axis=1).astype(jnp.bfloat16)
    value_means = jnp.mean(value_blocks.astype(jnp.float32), axis=1).astype(jnp.bfloat16)
    means = lax.all_gather(
        jnp.concatenate((key_means, value_means), axis=1), "ctx", axis=0, tiled=True
    )

    by_row = jnp.concatenate(
        (jnp.transpose(key_blocks, (1, 0, 2)), jnp.transpose(value_blocks, (1, 0, 2))), axis=0
    )
    asked = jnp.concatenate((pair_keys // block_count, pair_keys % block_count), axis=1)
    asked = jnp.pad(asked.astype(jnp.bfloat16), ((0, 0), (0, HD - 2 * pair_slots)))
    asked = jnp.broadcast_to(asked[None], (devices, block_count, HD))
    spread = lax.all_to_all(
        jnp.concatenate((by_row, asked), axis=2), "ctx", split_axis=0, concat_axis=0, tiled=True
    )
    table = spread[:, :, :columns].reshape(blocks, columns)
    asked = spread[:, :, columns : columns + 2 * pair_slots].astype(jnp.int32)
    wanted = asked[:, :, :pair_slots] * block_count + asked[:, :, pair_slots:]
    choose = wanted.reshape(-1, 1) == jnp.arange(blocks, dtype=jnp.int32)[None, :]
    chosen = jnp.dot(choose.astype(jnp.bfloat16), table, preferred_element_type=jnp.float32)
    chosen = chosen.astype(jnp.bfloat16).reshape(devices, block_count * pair_slots, columns)
    got = lax.all_to_all(chosen, "ctx", split_axis=0, concat_axis=0, tiled=True)
    return attend(queries, got, means, pair_keys, pair_count)


def solution(mesh):
    placed = (P("ctx", "head"), P("ctx", "head"), P("ctx", "head"), P("ctx", None), P("ctx"))
    return jax.shard_map(
        body, mesh=mesh, in_specs=placed, out_specs=P("ctx", "head"), check_vma=False
    )
```

time: 595 us -> 157 us (0.26); the launches traced: 585 us -> 156 us
  blocking collectives: 320 us -> 34.7 us
  local copies, waits for them, and re-layouts: 92.1 us -> 2.21 us
  starting transfers between devices: 46.2 us -> 6.44 us
  matrix products: 27.2 us -> 3.28 us
  other arithmetic: 16.7 us -> 3.75 us
  between operations: 0.63 us -> 13.5 us
  Pallas kernels: 0 us -> 7.88 us
    all_gather x2 -> x0, blocking collectives: 320 us -> none  [the longest x1 270 us: body(): mean_keys = lax.all_gather(key_means, 'ctx', axis=0, tiled=True)]
    all_gather x0 -> x1, waiting for transfers between devices: none -> 83.9 us  [body(): lax.all_gather(jnp.concatenate((key_means, value_means), axis=1), 'ctx',...]
    all_to_all x5 -> x1, waiting for transfers between devices: 82.6 us -> 0.01 us  [body(): got = lax.all_to_all(chosen, 'ctx', split_axis=0, concat_axis=0, tiled=True)]
    all_to_all x5 -> x1, starting transfers between devices: 46.2 us -> 6.39 us  [body(): got = lax.all_to_all(chosen, 'ctx', split_axis=0, concat_axis=0, tiled=True)]
    all_to_all x0 -> x1, blocking collectives: none -> 34.7 us  [body(): lax.all_to_all(jnp.concatenate((by_row, asked), axis=2), 'ctx', split_axi...]
    gather x6 -> x0, local copies, waits for them, and re-layouts: 28.4 us -> none  [the longest x2 16.4 us: body(): local_blocks = key_value[requested]]
    another operation x4 -> x0, local copies, waits for them, and re-layouts: 25.7 us -> none  [the longest x1 13.1 us: body(): local_blocks[:, :, 0]]
    dot_general x3 -> x1, matrix products: 25.7 us -> 3.28 us  [body(): jnp.dot(choose.astype(jnp.bfloat16), table, preferred_element_type=jnp.fl...]
  transfers between devices with their start and end apart: 5 -> 2, of which waited for: 2 -> 1; matrix products, arithmetic and copies ran while one was open for 16% -> 1% of each run, Pallas kernels for 0% -> 0%
where the time goes in v1:
time: 157 us; the launch traced here: 156 us
  waiting for transfers between devices  83.9 us (53%)
  blocking collectives  34.7 us (22%)
  between operations  13.5 us (9%)
  Pallas kernels  7.88 us (5%)
  starting transfers between devices  6.44 us (4%)
  other arithmetic  3.75 us (2%)
  matrix products  3.28 us (2%)
  local copies, waits for them, and re-layouts  2.21 us (1%)
    all_gather x1, waiting for transfers between devices, body(): lax.all_gather(jnp.concatenate((key_means, value_means), axis=1), 'ctx',...  83.9 us
    all_to_all x1, blocking collectives, body(): lax.all_to_all(jnp.concatenate((by_row, asked), axis=2), 'ctx', split_axi...  34.7 us
    pallas_call x1, Pallas kernels, attend(): pl.pallas_call(kernel, grid_spec=grid_spec, out_shape=jax.ShapeDtypeStruc...  7.88 us
    all_to_all x1, starting transfers between devices, body(): got = lax.all_to_all(chosen, 'ctx', split_axis=0, concat_axis=0, tiled=True)  6.39 us
    dot_general x1, matrix products, body(): jnp.dot(choose.astype(jnp.bfloat16), table, preferred_element_type=jnp.fl...  3.28 us
  transfers between devices with their start and end apart: 2, of which 1 were waited for; matrix products, arithmetic and copies ran while one was open for 1% of the time, Pallas kernels for 0%

profile of v1, /device:TPU:8, one launch (start us, length us, event | category | flops | bytes accessed | tf_op | source)
XLA Modules:
  0.0 155.6 jit_solution(15660545655486482677)
XLA Ops:
  6.5 0.7 fusion.3
  7.2 0.1 copy.17
  7.4 1.1 pad_maximum_fusion
  8.5 0.4 copy.16
  9.0 34.7 %all_to_all.10 = bf16[64,8,768]{2,1,0:T(8,128)(2,1)S(1)} all-to-all(bf16[64,8,768]{2,1,0:T(8,128)(2,1)S(1)} %copy.16), channel_id=1, replica_groups=mesh['ctx'=64,'head'=4] {'ctx'}, dimensions={0} | all-to-all | bytes 1572864 | tf_op jit(solution)/shard_map/all_to_all | solution.py:133
  43.6 0.1 slice_add_fusion
  43.8 0.2 eq.17
  43.9 3.3 %fusion.1 = bf16[2048,640]{1,0:T(8,128)(2,1)} fusion(s32[2048]{0:T(1024)S(1)} %eq.17, bf16[64,8,768]{2,1,0:T(8,128)(2,1)S(1)} %all_to_all.10), kind=kOutput, calls=%fused_computation.2 | convolution fusion | flops 1344536576 | bytes 3284992 | tf_op jit(solution)/shard_map/dot_general | solution.py:140
  47.2 0.0 copy-start.3
  47.2 0.0 copy-start.4
  47.2 0.0 copy-start.1
  47.2 0.0 copy-start.2
  47.2 6.4 %all-to-all-start.1 = ((bf16[64,32,640]{2,1,0:T(8,128)(2,1)}), bf16[64,32,640]{2,1,0:T(8,128)(2,1)S(1)}, u32[]{:S(2)}, u32[]{:S(2)}) async-start(bf16[64,32,640]{2,1,0:T(8,128)(2,1)} %bitcast.12), calls=%async_computation.1 | async-start | bytes 5242880 | tf_op jit(solution)/shard_map/all_to_all | solution.py:142
  53.6 0.0 all-gather.2.cloned.1.call-start
  53.7 0.0 copy-done.3
  53.7 0.1 convert_reduce_fusion
  53.8 1.1 convert_reduce_fusion.1
  54.9 0.6 pad_maximum_fusion.1
  55.5 0.0 all-gather.2.cloned.1.call-update
  55.5 0.0 copy-done.4
  55.5 0.1 copy.14
  55.6 0.1 reshape.18.refs_0_
  55.7 83.9 %all-gather.2.cloned.1.call-done.refs_4_.refs_5_ = bf16[512,1280]{1,0:T(8,128)(2,1)} async-done(((bf16[8,1280]{1,0:T(8,128)(2,1)}), bf16[512,1280]{1,0:T(8,128)(2,1)}) %all-gather.2.cloned.1.call-update) | async-done | bytes 1310736 | tf_op jit(solution)/shard_map/all_gather | solution.py:123
  139.6 0.0 all-to-all-done.1.refs_3_
  139.6 0.0 copy-done.1
  139.6 0.0 copy-done.2
  139.6 0.0 copy-start
  139.6 1.3 copy-done
  140.9 7.9 %shard_map.55 = bf16[256,640]{1,0:T(8,128)(2,1)} custom-call(s32[32]{0:T(128)S(1)} %reshape.18.refs_0_, s32[8]{0:T(128)S(1)} %copy-done.2, bf16[256,640]{1,0:T(8,128)(2,1)S(1)} %copy-done.1, bf16[64,32,640]{2,1,0:T(8,128)(2,1)S(1)} %all-to-all-done.1.refs_3_, bf16[512,1280]{1,0:T(8,128)(2,1)S(1)} %copy-done, bf16[512,1280]{1,0:T(8,128)(2,1)S(1)} %copy-done), custom_call_target="tpu_custom_call" | custom-call | flops 671088640 | bytes 8388608 | tf_op jit(solution)/shard_map/pallas_call | solution.py:98
  (5 shorter events, 0.1 us)
Async XLA Ops:
  47.2 6.5 %copy-start.3 = (bf16[256,640]{1,0:T(8,128)(2,1)S(1)}, bf16[256,640]{1,0:T(8,128)(2,1)}, u32[]{:S(2)}) copy-start(bf16[256,640]{1,0:T(8,128)(2,1)} %param.7) | copy-start | bytes 983044
  47.2 8.3 %copy-start.4 = (s32[8,4]{0,1:T(4,128)S(1)}, s32[8,4]{0,1:T(4,128)}, u32[]{:S(2)}) copy-start(s32[8,4]{0,1:T(4,128)} %param.8) | copy-start | bytes 388
  47.2 92.4 %copy-start.1 = (bf16[256,640]{1,0:T(8,128)(2,1)S(1)}, bf16[256,640]{1,0:T(8,128)(2,1)}, u32[]{:S(2)}) copy-start(bf16[256,640]{1,0:T(8,128)(2,1)} %refs_2_.1) | copy-start | bytes 983044
  47.2 92.4 %copy-start.2 = (s32[8]{0:T(128)S(1)}, s32[8]{0:T(128)}, u32[]{:S(2)}) copy-start(s32[8]{0:T(128)} %refs_1_.1) | copy-start | bytes 100
  47.2 92.3 %all-to-all-start.1 = ((bf16[64,32,640]{2,1,0:T(8,128)(2,1)}), bf16[64,32,640]{2,1,0:T(8,128)(2,1)S(1)}, u32[]{:S(2)}, u32[]{:S(2)}) async-start(bf16[64,32,640]{2,1,0:T(8,128)(2,1)} %bitcast.12), calls=%async_computation.1 | async-start | bytes 5242880 | tf_op jit(solution)/shard_map/all_to_all | solution.py:142
  53.6 85.9 %all-gather.2.cloned.1.call-start = ((), (), s32[]{:S(2)}) async-start(), calls=%async_computation.2 | async-start | bytes 1331200 | tf_op jit(solution)/shard_map/all_gather | solution.py:123
  139.6 1.3 copy-start
Sparse Core Ops, SparseCore 0:
  57.2 82.3 all-gather.1
